TPU v7x, 32 devices: a whole 2x2x4 slice. The times are simulated.
32 devices in a mesh: dp: 16 (over z, x, core), tensor: 2 (over y).
Axes of the slice: x: 2, y: 2, z: 4, core: 2. Of those that a mesh axis runs over, the one named last changes fastest.
Arguments:
- layer_in: bfloat16 [4096, 1024], P(('dp', 'tensor')), may hold values from -6 to 6
- seq_lengths: int32 [16, 4], P('dp'), may hold values from 1 to 206, as said below
- attn_gain: float32 [1024], replicated, may hold values from 0.1 to 1.9
- query_gain: float32 [128], replicated, may hold values from 0.1 to 1.9
- key_gain: float32 [128], replicated, may hold values from 0.1 to 1.9
- query_weight: bfloat16 [1024, 2048], P('dp', 'tensor'), may hold values from -0.1875 to 0.1875
- key_matrix: bfloat16 [1024, 1024], P('dp', 'tensor'), may hold values from -0.1875 to 0.1875
- value_matrix: bfloat16 [1024, 1024], P('dp', 'tensor'), may hold values from -0.1875 to 0.1875
- output_weight: bfloat16 [2048, 1024], P('tensor', 'dp'), may hold values from -0.75 to 0.75
- mlp_gain: float32 [1024], replicated, may hold values from 0.1 to 1.9
- gate_weight: bfloat16 [1024, 3072], P('dp', 'tensor'), may hold values from -0.1875 to 0.1875
- up_weight: bfloat16 [1024, 3072], P('dp', 'tensor'), may hold values from -0.1875 to 0.1875
- down_weight: bfloat16 [3072, 1024], P('tensor', 'dp'), may hold values from -0.109375 to 0.109375
- out_grad: bfloat16 [4096, 1024], P(('dp', 'tensor')), may hold values from -6 to 6
Outputs:
- layer_out: bfloat16 [4096, 1024], P(('dp', 'tensor'))
- input_grad: bfloat16 [4096, 1024], P(('dp', 'tensor'))
- attn_gain_grad: float32 [1024], replicated
- query_gain_grad: float32 [128], replicated
- key_gain_grad: float32 [128], replicated
- query_weight_grad: float32 [1024, 2048], P('dp', 'tensor')
- key_weight_grad: float32 [1024, 1024], P('dp', 'tensor')
- value_weight_grad: float32 [1024, 1024], P('dp', 'tensor')
- output_weight_grad: float32 [2048, 1024], P('tensor', 'dp')
- mlp_gain_grad: float32 [1024], replicated
- gate_weight_grad: float32 [1024, 3072], P('dp', 'tensor')
- up_weight_grad: float32 [1024, 3072], P('dp', 'tensor')
- down_weight_grad: float32 [3072, 1024], P('tensor', 'dp')
Inputs may be any that keep to these rules, and one draw needn't show every extreme that they name: `seq_lengths`: in each group the 4 lengths are positive and sum to at most 256, and to exactly 256 in some group; slots after the last sequence of a group are padding; the most is reached in some group.
All inputs are finite; a program needn't handle non-finite values.
Results may differ from a plain program's by a relative error of at most 0.018.
Values may be sent and summed in bfloat16 or wider, within the bound.
A program may use at most 128 MiB of HBM per device.

v0:
```python
import jax
import jax.numpy as jnp
from jax import lax
from jax.sharding import PartitionSpec as P

HEAD_SIZE = 128


EPS = 1e-06
NEG = -1e30
ROPE_BASE = 1000000.0


def normalize(v, gain):
    return v * lax.rsqrt(jnp.mean(v * v, -1, keepdims=True) + EPS) * gain


def layout(lengths_row, count):
    slots = jnp.arange(count, dtype=jnp.int32)
    ends = jnp.cumsum(lengths_row)
    seg = jnp.sum((slots[:, None] >= ends[None, :]).astype(jnp.int32), 1)
    starts = jnp.concatenate([jnp.zeros((1,), jnp.int32), ends])
    which = seg[:, None] == jnp.arange(starts.shape[0], dtype=jnp.int32)[None, :]
    start_of = jnp.sum(jnp.where(which, starts[None, :], 0), 1)
    return (slots, seg, slots - start_of)


def rotate(v, cosine, sine):
    half = v.shape[-1] // 2
    first = v[..., :half]
    second = v[..., half:]
    cos_b = cosine[:, None, :]
    sin_b = sine[:, None, :]
    return jnp.concatenate([first * cos_b - second * sin_b, second * cos_b + first * sin_b], -1)


def head_prep(raw, gain, cosine, sine, heads):
    shaped = raw.reshape(raw.shape[0], heads, HEAD_SIZE)
    return rotate(normalize(shaped, gain), cosine, sine)


def matrix_product(a, b):
    return jnp.dot(a, b, preferred_element_type=jnp.float32)


def by_rows(a, b):
    return lax.dot_general(a, b, (((0,), (0,)), ((), ())), preferred_element_type=jnp.float32)


def by_cols(a, b):
    return lax.dot_general(a, b, (((1,), (1,)), ((), ())), preferred_element_type=jnp.float32)


def shards(
    layer_in,
    seq_lengths,
    attn_gain,
    query_gain,
    key_gain,
    query_weight,
    key_matrix,
    value_matrix,
    output_weight,
    mlp_gain,
    gate_weight,
    up_weight,
    down_weight,
    out_grad,
):
    bf = jnp.bfloat16
    q_heads = query_weight.shape[1] // HEAD_SIZE
    kv_heads = key_matrix.shape[1] // HEAD_SIZE
    group = q_heads // kv_heads
    scale = HEAD_SIZE ** (-0.5)
    wq, key_projection_weight, value_projection_weight, wo = (
        lax.all_gather(query_weight, "dp", axis=0, tiled=True),
        lax.all_gather(key_matrix, "dp", axis=0, tiled=True),
        lax.all_gather(value_matrix, "dp", axis=0, tiled=True),
        lax.all_gather(output_weight, "dp", axis=1, tiled=True),
    )
    wg, wu, wd = (
        lax.all_gather(gate_weight, "dp", axis=0, tiled=True),
        lax.all_gather(up_weight, "dp", axis=0, tiled=True),
        lax.all_gather(down_weight, "dp", axis=1, tiled=True),
    )
    residual = layer_in.astype(jnp.float32)
    first_activation = normalize(residual, attn_gain).astype(bf)
    a1_full = lax.all_gather(first_activation, "tensor", axis=0, tiled=True)
    count = a1_full.shape[0]
    slots, seg, pos = layout(seq_lengths[0], count)
    inv = ROPE_BASE ** (-2.0 * jnp.arange(HEAD_SIZE // 2, dtype=jnp.float32) / HEAD_SIZE)
    angle = pos.astype(jnp.float32)[:, None] * inv[None, :]
    cosine = jnp.cos(angle)
    sine = jnp.sin(angle)
    allowed = (seg[:, None] == seg[None, :]) & (slots[None, :] <= slots[:, None])
    q_raw = matrix_product(a1_full, wq)
    key_unrotated = matrix_product(a1_full, key_projection_weight)
    v_raw = matrix_product(a1_full, value_projection_weight)
    q_bf = (
        head_prep(q_raw, query_gain, cosine, sine, q_heads)
        .astype(bf)
        .reshape(count, kv_heads, group, HEAD_SIZE)
    )
    k_bf = head_prep(key_unrotated, key_gain, cosine, sine, kv_heads).astype(bf)
    v_bf = v_raw.astype(bf).reshape(count, kv_heads, HEAD_SIZE)

    def masked_scores():
        raw = jnp.einsum("qhgd,khd->hgqk", q_bf, k_bf, preferred_element_type=jnp.float32) * scale
        return jnp.where(allowed, raw, NEG)

    masked = masked_scores()
    top = jnp.max(masked, -1, keepdims=True)
    log_total = top + jnp.log(jnp.sum(jnp.exp(masked - top), -1, keepdims=True))
    probs_bf = jnp.exp(masked - log_total).astype(bf)
    attended = jnp.einsum("hgqk,khd->qhgd", probs_bf, v_bf, preferred_element_type=jnp.float32)
    attended_bf = attended.reshape(count, q_heads * HEAD_SIZE).astype(bf)
    attn_sum = lax.psum_scatter(
        matrix_product(attended_bf, wo).astype(jnp.bfloat16),
        "tensor",
        scatter_dimension=0,
        tiled=True,
    ).astype(jnp.float32)
    middle = residual + attn_sum
    a2_full = lax.all_gather(normalize(middle, mlp_gain).astype(bf), "tensor", axis=0, tiled=True)
    gate = matrix_product(a2_full, wg)
    upward = matrix_product(a2_full, wu)
    sigma = jax.nn.sigmoid(gate)
    act = (gate * sigma * upward).astype(bf)
    mlp_sum = lax.psum_scatter(
        matrix_product(act, wd).astype(jnp.bfloat16), "tensor", scatter_dimension=0, tiled=True
    ).astype(jnp.float32)
    layer_out = (middle + mlp_sum).astype(bf)
    wq, key_projection_weight, value_projection_weight, wo, wg, wu, wd = (
        lax.all_gather(query_weight, "dp", axis=0, tiled=True),
        lax.all_gather(key_matrix, "dp", axis=0, tiled=True),
        lax.all_gather(value_matrix, "dp", axis=0, tiled=True),
        lax.all_gather(output_weight, "dp", axis=1, tiled=True),
        lax.all_gather(gate_weight, "dp", axis=0, tiled=True),
        lax.all_gather(up_weight, "dp", axis=0, tiled=True),
        lax.all_gather(down_weight, "dp", axis=1, tiled=True),
    )
    dy_full = lax.all_gather(out_grad, "tensor", axis=0, tiled=True)
    d_act = by_cols(dy_full, wd)
    down_grad = by_rows(act, dy_full)
    d_gate = (d_act * upward * sigma * (1.0 + gate * (1.0 - sigma))).astype(bf)
    d_up = (d_act * gate * sigma).astype(bf)
    gate_grad = by_rows(a2_full, d_gate)
    up_grad = by_rows(a2_full, d_up)
    d_a2 = lax.psum_scatter(
        (by_cols(d_gate, wg) + by_cols(d_up, wu)).astype(jnp.bfloat16),
        "tensor",
        scatter_dimension=0,
        tiled=True,
    ).astype(jnp.float32)
    _, pull_mid = jax.vjp(normalize, middle, mlp_gain)
    d_mid_norm, mlp_gain_part = pull_mid(d_a2)
    d_middle = out_grad.astype(jnp.float32) + d_mid_norm
    dh_full = lax.all_gather(d_middle.astype(bf), "tensor", axis=0, tiled=True)
    output_grad = by_rows(attended_bf, dh_full)
    d_att = by_cols(dh_full, wo).astype(bf).reshape(count, kv_heads, group, HEAD_SIZE)
    probs = jnp.exp(masked_scores() - log_total)
    probs_again = probs.astype(bf)
    d_probs = jnp.einsum("qhgd,khd->hgqk", d_att, v_bf, preferred_element_type=jnp.float32)
    delta = jnp.sum(d_probs * probs, -1, keepdims=True)
    d_scores = (probs * (d_probs - delta)).astype(bf)
    d_q_rot = (
        jnp.einsum("hgqk,khd->qhgd", d_scores, k_bf, preferred_element_type=jnp.float32) * scale
    ).reshape(count, q_heads, HEAD_SIZE)
    d_k_rot = (
        jnp.einsum("hgqk,qhgd->khd", d_scores, q_bf, preferred_element_type=jnp.float32) * scale
    )
    d_v_raw = (
        jnp.einsum("hgqk,qhgd->khd", probs_again, d_att, preferred_element_type=jnp.float32)
        .reshape(count, kv_heads * HEAD_SIZE)
        .astype(bf)
    )
    _, pull_query = jax.vjp(
        lambda raw, gain: head_prep(raw, gain, cosine, sine, q_heads), q_raw, query_gain
    )
    d_q_raw, query_gain_part = pull_query(d_q_rot)
    _, pull_key = jax.vjp(
        lambda raw, gain: head_prep(raw, gain, cosine, sine, kv_heads), key_unrotated, key_gain
    )
    d_k_raw, key_gain_part = pull_key(d_k_rot)
    d_q_bf = d_q_raw.astype(bf)
    d_k_bf = d_k_raw.astype(bf)
    query_grad = by_rows(a1_full, d_q_bf)
    key_grad = by_rows(a1_full, d_k_bf)
    value_grad = by_rows(a1_full, d_v_raw)
    d_a1_part = (
        by_cols(d_q_bf, wq)
        + by_cols(d_k_bf, key_projection_weight)
        + by_cols(d_v_raw, value_projection_weight)
    )
    d_a1 = lax.psum_scatter(
        d_a1_part.astype(jnp.bfloat16), "tensor", scatter_dimension=0, tiled=True
    ).astype(jnp.float32)
    summed = (
        lax.psum_scatter(query_grad, "dp", scatter_dimension=0, tiled=True),
        lax.psum_scatter(key_grad, "dp", scatter_dimension=0, tiled=True),
        lax.psum_scatter(value_grad, "dp", scatter_dimension=0, tiled=True),
        lax.psum_scatter(output_grad, "dp", scatter_dimension=1, tiled=True),
        lax.psum_scatter(gate_grad, "dp", scatter_dimension=0, tiled=True),
        lax.psum_scatter(up_grad, "dp", scatter_dimension=0, tiled=True),
        lax.psum_scatter(down_grad, "dp", scatter_dimension=1, tiled=True),
    )
    attn_grads = summed[:4]
    mlp_grads = summed[4:]
    _, pull_in = jax.vjp(normalize, residual, attn_gain)
    d_in_norm, attn_gain_part = pull_in(d_a1)
    input_grad = (d_middle + d_in_norm).astype(bf)
    gains = lax.psum(
        (attn_gain_part, query_gain_part, key_gain_part, mlp_gain_part), ("dp", "tensor")
    )
    return (
        layer_out,
        input_grad,
        gains[0],
        gains[1],
        gains[2],
        attn_grads[0],
        attn_grads[1],
        attn_grads[2],
        attn_grads[3],
        gains[3],
        mlp_grads[0],
        mlp_grads[1],
        mlp_grads[2],
    )


def solution(mesh):
    placed = (
        P(("dp", "tensor"), None),
        P("dp", None),
        P(),
        P(),
        P(),
        P("dp", "tensor"),
        P("dp", "tensor"),
        P("dp", "tensor"),
        P("tensor", "dp"),
        P(),
        P("dp", "tensor"),
        P("dp", "tensor"),
        P("tensor", "dp"),
        P(("dp", "tensor"), None),
    )
    return jax.shard_map(
        shards,
        mesh=mesh,
        in_specs=placed,
        out_specs=(
            P(("dp", "tensor"), None),
            P(("dp", "tensor"), None),
            P(),
            P(),
            P(),
            P("dp", "tensor"),
            P("dp", "tensor"),
            P("dp", "tensor"),
            P("tensor", "dp"),
            P(),
            P("dp", "tensor"),
            P("dp", "tensor"),
            P("tensor", "dp"),
        ),
        check_vma=False,
    )
```

profile of v0, /device:TPU:0, one launch (start us, length us, event | category | flops | bytes accessed | tf_op | source)
XLA Modules:
  0.0 991.2 jit_solution(3774957464058774135)
XLA Ops:
  14.0 9.9 %all_gather.40 = bf16[256,1024]{1,0:T(8,128)(2,1)S(1)} all-gather(bf16[128,1024]{1,0:T(8,128)(2,1)S(1)} %fusion.14), channel_id=1, replica_groups=mesh['dp'=16,'tensor'=2] {'tensor'}, dimensions={0}, use_global_device_ids=true | all-gather | bytes 786432 | tf_op jit(solution)/shard_map/all_gather | solution.py:88
  24.5 26.3 %all-gather.8.cloned.1.call-done = bf16[1024,512]{1,0:T(8,128)(2,1)} async-done(((bf16[64,512]{1,0:T(8,128)(2,1)}), bf16[1024,512]{1,0:T(8,128)(2,1)}) %all-gather.8.cloned.1.call-update) | async-done | bytes 1048592 | tf_op jit(solution)/shard_map/all_gather | solution.py:78
  53.3 36.6 %all-gather.10.cloned.1.call-done = bf16[1024,512]{1,0:T(8,128)(2,1)} async-done(((bf16[64,512]{1,0:T(8,128)(2,1)}), bf16[1024,512]{1,0:T(8,128)(2,1)}) %all-gather.10.cloned.1.call-update) | async-done | bytes 1048592 | tf_op jit(solution)/shard_map/all_gather | solution.py:77
  93.4 39.0 %all-gather.12.cloned.1.call-done = bf16[1024,1024]{1,0:T(8,128)(2,1)} async-done(((bf16[64,1024]{1,0:T(8,128)(2,1)}), bf16[1024,1024]{1,0:T(8,128)(2,1)}) %all-gather.12.cloned.1.call-update) | async-done | bytes 2097168 | tf_op jit(solution)/shard_map/all_gather | solution.py:76
  139.3 35.3 %all-gather.14.cloned.1.call-done = bf16[1024,1024]{0,1:T(8,128)(2,1)} async-done(((bf16[1024,64]{0,1:T(8,128)(2,1)}), bf16[1024,1024]{0,1:T(8,128)(2,1)}) %all-gather.14.cloned.1.call-update) | async-done | bytes 2097168 | tf_op jit(solution)/shard_map/all_gather | solution.py:79
  180.1 16.1 %all_gather.49 = bf16[256,1024]{1,0:T(8,128)(2,1)} all-gather(bf16[128,1024]{1,0:T(8,128)(2,1)} %param.27), channel_id=1, replica_groups=mesh['dp'=16,'tensor'=2] {'tensor'}, dimensions={0}, use_global_device_ids=true | all-gather | bytes 786432 | tf_op jit(solution)/shard_map/all_gather | solution.py:142
  200.4 8.5 all_gather.45
  208.9 34.1 %all-gather.18.cloned.1.call-done = bf16[1024,1536]{1,0:T(8,128)(2,1)} async-done(((bf16[64,1536]{1,0:T(8,128)(2,1)}), bf16[1024,1536]{1,0:T(8,128)(2,1)}) %all-gather.18.cloned.1.call-update) | async-done | bytes 3145744 | tf_op jit(solution)/shard_map/all_gather | solution.py:83
  243.0 4.2 fusion.50
  247.1 42.4 %all-gather.16.cloned.1.call-done = bf16[1024,1536]{1,0:T(8,128)(2,1)} async-done(((bf16[64,1536]{1,0:T(8,128)(2,1)}), bf16[1024,1536]{1,0:T(8,128)(2,1)}) %all-gather.16.cloned.1.call-update) | async-done | bytes 3145744 | tf_op jit(solution)/shard_map/all_gather | solution.py:82
  289.5 4.2 fusion.49
  293.7 42.4 %all-gather.20.cloned.1.call-done = bf16[1536,1024]{0,1:T(8,128)(2,1)} async-done(((bf16[1536,64]{0,1:T(8,128)(2,1)}), bf16[1536,1024]{0,1:T(8,128)(2,1)}) %all-gather.20.cloned.1.call-update) | async-done | bytes 3145744 | tf_op jit(solution)/shard_map/all_gather | solution.py:84
  336.1 5.4 multiply_convert_fusion
  346.0 13.3 %reduce-scatter.16.cloned.1.call-done = bf16[128,1024]{1,0:T(8,128)(2,1)} async-done(((bf16[256,1024]{1,0:T(8,128)(2,1)}), bf16[128,1024]{1,0:T(8,128)(2,1)}) %reduce-scatter.16.cloned.1.call-update) | async-done | bytes 262160 | tf_op jit(solution)/shard_map/reduce_scatter | solution.py:149
  364.0 8.7 all_gather.50
  401.9 3.8 convolution_convert_fusion.3
  432.8 39.6 %all-reduce.4 = (f32[1024]{0:T(1024)}, f32[128]{0:T(128)}, f32[128]{0:T(128)}, f32[1024]{0:T(1024)}) all-reduce(f32[1024]{0:T(1024)S(1)} %get-tuple-element.19, f32[128]{0:T(128)S(1)} %copy-done.62, f32[128]{0:T(128)S(1)} %copy-done.61, f32[1024]{0:T(1024)S(1)} %copy-done.50), channel_id=1, replica_groups=mesh['dp'=16,'tensor'=2] {'dp','tensor'}, use_global_device_ids=true, to_apply=%region_19.20 | all-reduce | flops 2304 | bytes 18432 | tf_op jit(solution)/shard_map/psum | solution.py:212
  474.8 25.2 %reduce-scatter.24.cloned.1.call-done = f32[64,512]{1,0:T(8,128)} async-done(((f32[1024,512]{1,0:T(8,128)}), f32[64,512]{1,0:T(8,128)}) %reduce-scatter.24.cloned.1.call-update) | async-done | bytes 131088 | tf_op jit(solution)/shard_map/reduce_scatter | solution.py:201
  499.9 65.4 %reduce-scatter.22.cloned.1.call-done = f32[64,512]{1,0:T(8,128)} async-done(((f32[1024,512]{1,0:T(8,128)}), f32[64,512]{1,0:T(8,128)}) %reduce-scatter.22.cloned.1.call-update) | async-done | bytes 131088 | tf_op jit(solution)/shard_map/reduce_scatter | solution.py:200
  565.3 76.1 %reduce-scatter.20.cloned.1.call-done = f32[64,1024]{1,0:T(8,128)} async-done(((f32[1024,1024]{1,0:T(8,128)}), f32[64,1024]{1,0:T(8,128)}) %reduce-scatter.20.cloned.1.call-update) | async-done | bytes 262160 | tf_op jit(solution)/shard_map/reduce_scatter | solution.py:199
  641.4 76.3 %reduce-scatter.26.cloned.1.call-done = f32[1024,64]{0,1:T(8,128)} async-done(((f32[1024,1024]{0,1:T(8,128)}), f32[1024,64]{0,1:T(8,128)}) %reduce-scatter.26.cloned.1.call-update) | async-done | bytes 262160 | tf_op jit(solution)/shard_map/reduce_scatter | solution.py:202
  717.6 88.6 %reduce-scatter.30.cloned.1.call-done = f32[64,1536]{1,0:T(8,128)} async-done(((f32[1024,1536]{1,0:T(8,128)}), f32[64,1536]{1,0:T(8,128)}) %reduce-scatter.30.cloned.1.call-update) | async-done | bytes 393232 | tf_op jit(solution)/shard_map/reduce_scatter | solution.py:204
  806.3 89.3 %reduce-scatter.28.cloned.1.call-done = f32[64,1536]{1,0:T(8,128)} async-done(((f32[1024,1536]{1,0:T(8,128)}), f32[64,1536]{1,0:T(8,128)}) %reduce-scatter.28.cloned.1.call-update) | async-done | bytes 393232 | tf_op jit(solution)/shard_map/reduce_scatter | solution.py:203
  895.6 88.8 %reduce-scatter.32.cloned.1.call-done = f32[1536,64]{0,1:T(8,128)} async-done(((f32[1536,1024]{0,1:T(8,128)}), f32[1536,64]{0,1:T(8,128)}) %reduce-scatter.32.cloned.1.call-update) | async-done | bytes 393232 | tf_op jit(solution)/shard_map/reduce_scatter | solution.py:205
  (250 shorter events, 96.8 us)
Async XLA Ops:
  7.2 43.7 %all-gather.8.cloned.1.call-start = ((), (), s32[]{:S(2)}) async-start(), calls=%async_computation.11 | async-start | bytes 1114112 | tf_op jit(solution)/shard_map/all_gather | solution.py:78
  7.9 82.0 %all-gather.10.cloned.1.call-start = ((), (), s32[]{:S(2)}) async-start(), calls=%async_computation.12 | async-start | bytes 1114112 | tf_op jit(solution)/shard_map/all_gather | solution.py:77
  8.7 123.8 %all-gather.12.cloned.1.call-start = ((), (), s32[]{:S(2)}) async-start(), calls=%async_computation.13 | async-start | bytes 2228224 | tf_op jit(solution)/shard_map/all_gather | solution.py:76
  9.4 165.2 %all-gather.14.cloned.1.call-start = ((), (), s32[]{:S(2)}) async-start(), calls=%async_computation.14 | async-start | bytes 2228224 | tf_op jit(solution)/shard_map/all_gather | solution.py:79
  10.0 187.1 %reduce-scatter.12.cloned.1.call-start = ((), (), s32[]{:S(2)}) async-start(), calls=%async_computation.15 | async-start | bytes 786432 | tf_op jit(solution)/shard_map/reduce_scatter | solution.py:117
  24.0 108.4 %copy-start = (bf16[256,1024]{1,0:T(8,128)(2,1)}, bf16[256,1024]{1,0:T(8,128)(2,1)S(1)}, u32[]{:S(2)}) copy-start(bf16[256,1024]{1,0:T(8,128)(2,1)S(1)} %all_gather.40) | copy-start | bytes 1572868
  24.5 111.4 %copy-start.18 = (f32[256,64]{1,0:T(8,128)}, f32[256,64]{1,0:T(8,128)S(1)}, u32[]{:S(2)}) copy-start(f32[256,64]{1,0:T(8,128)S(1)} %get-tuple-element.41) | copy-start | bytes 196612
  92.2 42.5 %copy-start.48 = (f32[256,4]{0,1:T(4,128)}, f32[256,4]{0,1:T(4,128)S(1)}, u32[]{:S(2)}) copy-start(f32[256,4]{0,1:T(4,128)S(1)} %copy.153) | copy-start | bytes 12292
  92.2 42.5 %copy-start.45 = (f32[256,4]{0,1:T(4,128)}, f32[256,4]{0,1:T(4,128)S(1)}, u32[]{:S(2)}) copy-start(f32[256,4]{0,1:T(4,128)S(1)} %fusion.39) | copy-start | bytes 12292
  178.0 65.0 %all-gather.18.cloned.1.call-start = ((), (), s32[]{:S(2)}) async-start(), calls=%async_computation.17 | async-start | bytes 3342336 | tf_op jit(solution)/shard_map/all_gather | solution.py:83
  178.6 111.0 %all-gather.16.cloned.1.call-start = ((), (), s32[]{:S(2)}) async-start(), calls=%async_computation.16 | async-start | bytes 3342336 | tf_op jit(solution)/shard_map/all_gather | solution.py:82
  179.3 156.8 %all-gather.20.cloned.1.call-start = ((), (), s32[]{:S(2)}) async-start(), calls=%async_computation.18 | async-start | bytes 3342336 | tf_op jit(solution)/shard_map/all_gather | solution.py:84
  180.1 179.2 %reduce-scatter.16.cloned.1.call-start = ((), (), s32[]{:S(2)}) async-start(), calls=%async_computation.20 | async-start | bytes 786432 | tf_op jit(solution)/shard_map/reduce_scatter | solution.py:149
  345.8 85.3 %reduce-scatter.18.cloned.1.call-start = ((), (), s32[]{:S(2)}) async-start(), calls=%async_computation.21 | async-start | bytes 786432 | tf_op jit(solution)/shard_map/reduce_scatter | solution.py:195
  401.9 70.6 %reduce-scatter.14.cloned.1.call-start = ((), (), s32[]{:S(2)}) async-start(), calls=%async_computation.19 | async-start | bytes 786432 | tf_op jit(solution)/shard_map/reduce_scatter | solution.py:129
  405.7 94.2 %reduce-scatter.24.cloned.1.call-start = ((), (), s32[]{:S(2)}) async-start(), calls=%async_computation.24 | async-start | bytes 2228224 | tf_op jit(solution)/shard_map/reduce_scatter | solution.py:201
  407.6 157.7 %reduce-scatter.22.cloned.1.call-start = ((), (), s32[]{:S(2)}) async-start(), calls=%async_computation.23 | async-start | bytes 2228224 | tf_op jit(solution)/shard_map/reduce_scatter | solution.py:200
  409.6 231.8 %reduce-scatter.20.cloned.1.call-start = ((), (), s32[]{:S(2)}) async-start(), calls=%async_computation.22 | async-start | bytes 4456448 | tf_op jit(solution)/shard_map/reduce_scatter | solution.py:199
  412.5 305.2 %reduce-scatter.26.cloned.1.call-start = ((), (), s32[]{:S(2)}) async-start(), calls=%async_computation.25 | async-start | bytes 4456448 | tf_op jit(solution)/shard_map/reduce_scatter | solution.py:202
  416.5 389.8 %reduce-scatter.30.cloned.1.call-start = ((), (), s32[]{:S(2)}) async-start(), calls=%async_computation.27 | async-start | bytes 6684672 | tf_op jit(solution)/shard_map/reduce_scatter | solution.py:204
  421.5 474.1 %reduce-scatter.28.cloned.1.call-start = ((), (), s32[]{:S(2)}) async-start(), calls=%async_computation.26 | async-start | bytes 6684672 | tf_op jit(solution)/shard_map/reduce_scatter | solution.py:203
  426.3 558.1 %reduce-scatter.32.cloned.1.call-start = ((), (), s32[]{:S(2)}) async-start(), calls=%async_computation.28 | async-start | bytes 6684672 | tf_op jit(solution)/shard_map/reduce_scatter | solution.py:205
  431.0 41.5 %copy-start.7 = (bf16[128,1024]{1,0:T(8,128)(2,1)S(1)}, bf16[128,1024]{1,0:T(8,128)(2,1)}, u32[]{:S(2)}) copy-start(bf16[128,1024]{1,0:T(8,128)(2,1)} %reduce-scatter.12.cloned.1.call-done) | copy-start | bytes 786436
  431.0 41.5 %copy-start.26 = (bf16[128,1024]{1,0:T(8,128)(2,1)S(1)}, bf16[128,1024]{1,0:T(8,128)(2,1)}, u32[]{:S(2)}) copy-start(bf16[128,1024]{1,0:T(8,128)(2,1)} %param.27) | copy-start | bytes 786436
  (61 other events, 369.2 us)
Sparse Core Ops, SparseCore 0:
  10.2 40.6 all-gather.7
  53.0 36.8 all-gather.9
  92.1 40.3 all-gather.11
  134.4 40.1 all-gather.13
  178.1 18.9 reduce-scatter.11
  199.5 43.4 all-gather.17
  245.5 43.9 all-gather.15
  292.1 43.9 all-gather.19
  345.9 13.3 reduce-scatter.15
  402.0 14.5 reduce-scatter.17
  418.9 14.5 reduce-scatter.13
  437.7 62.2 reduce-scatter.23
  504.7 60.5 reduce-scatter.21
  569.6 71.7 reduce-scatter.19
  646.1 71.4 reduce-scatter.25
  722.0 84.2 reduce-scatter.29
  811.1 84.4 reduce-scatter.27
  900.0 84.3 reduce-scatter.31
where the time goes:
time: 992 us; the launch traced here: 991 us
  waiting for transfers between devices  785 us (79%)
  blocking collectives  82.9 us (8%)
  matrix products  59.5 us (6%)
  other arithmetic  25.3 us (3%)
  local copies, waits for them, and re-layouts  22.8 us (2%)
  between operations  15.1 us (2%)
    reduce_scatter x1, waiting for transfers between devices, shards(): lax.psum_scatter(gate_grad, 'dp', scatter_dimension=0, tiled=True)  89.3 us
    reduce_scatter x1, waiting for transfers between devices, shards(): lax.psum_scatter(down_grad, 'dp', scatter_dimension=1, tiled=True)  88.8 us
    reduce_scatter x1, waiting for transfers between devices, shards(): lax.psum_scatter(up_grad, 'dp', scatter_dimension=0, tiled=True)  88.6 us
    reduce_scatter x1, waiting for transfers between devices, shards(): lax.psum_scatter(output_grad, 'dp', scatter_dimension=1, tiled=True)  76.3 us
    reduce_scatter x1, waiting for transfers between devices, shards(): lax.psum_scatter(query_grad, 'dp', scatter_dimension=0, tiled=True)  76.1 us
    reduce_scatter x1, waiting for transfers between devices, shards(): lax.psum_scatter(key_grad, 'dp', scatter_dimension=0, tiled=True)  65.4 us
    all_gather x1, waiting for transfers between devices, shards(): lax.all_gather(gate_weight, 'dp', axis=0, tiled=True)  42.4 us
    all_gather x1, waiting for transfers between devices, shards(): lax.all_gather(down_weight, 'dp', axis=1, tiled=True)  42.4 us
  transfers between devices with their start and end apart: 18, of which 16 were waited for; matrix products, arithmetic and copies ran while one was open for 6% of the time, Pallas kernels for 0%

commit v1 on v0

v1 whole, which is shorter than its diff:
```python
import jax
import jax.numpy as jnp
from jax import lax
from jax.sharding import PartitionSpec as P

HEAD_SIZE = 128


EPS = 1e-06
NEG = -1e30
ROPE_BASE = 1000000.0


def normalize(v, gain):
    return v * lax.rsqrt(jnp.mean(v * v, -1, keepdims=True) + EPS) * gain


def layout(lengths_row, slots):
    ends = jnp.cumsum(lengths_row)
    seg = jnp.sum((slots[:, None] >= ends[None, :]).astype(jnp.int32), 1)
    starts = jnp.concatenate([jnp.zeros((1,), jnp.int32), ends])
    which = seg[:, None] == jnp.arange(starts.shape[0], dtype=jnp.int32)[None, :]
    start_of = jnp.sum(jnp.where(which, starts[None, :], 0), 1)
    return (seg, slots - start_of)


def swap(v):
    return lax.ppermute(v, "tensor", [(0, 1), (1, 0)])


def pair_sum(part):
    other = swap(part).astype(jnp.float32)
    half = part.shape[0] // 2
    return part.astype(jnp.float32) + jnp.concatenate([other[half:], other[:half]], axis=0)


def rotate(v, cosine, sine):
    half = v.shape[-1] // 2
    first = v[..., :half]
    second = v[..., half:]
    cos_b = cosine[:, None, :]
    sin_b = sine[:, None, :]
    return jnp.concatenate([first * cos_b - second * sin_b, second * cos_b + first * sin_b], -1)


def head_prep(raw, gain, cosine, sine, heads):
    shaped = raw.reshape(raw.shape[0], heads, HEAD_SIZE)
    return rotate(normalize(shaped, gain), cosine, sine)


def matrix_product(a, b):
    return jnp.dot(a, b, preferred_element_type=jnp.float32)


def by_rows(a, b):
    return lax.dot_general(a, b, (((0,), (0,)), ((), ())), preferred_element_type=jnp.float32)


def by_cols(a, b):
    return lax.dot_general(a, b, (((1,), (1,)), ((), ())), preferred_element_type=jnp.float32)


def shards(
    layer_in,
    seq_lengths,
    attn_gain,
    query_gain,
    key_gain,
    query_weight,
    key_matrix,
    value_matrix,
    output_weight,
    mlp_gain,
    gate_weight,
    up_weight,
    down_weight,
    out_grad,
):
    bf = jnp.bfloat16
    f32 = jnp.float32
    q_heads = query_weight.shape[1] // HEAD_SIZE
    kv_heads = key_matrix.shape[1] // HEAD_SIZE
    group = q_heads // kv_heads
    scale = HEAD_SIZE ** (-0.5)
    own = layer_in.shape[0]
    count = 2 * own
    q_cols, k_cols, units = query_weight.shape[1], key_matrix.shape[1], gate_weight.shape[1]
    qkv_cols = q_cols + 2 * k_cols

    attn_pack = jnp.concatenate(
        [query_weight, key_matrix, value_matrix, output_weight.T], axis=1
    )
    mlp_pack = jnp.concatenate([gate_weight, up_weight, down_weight.T], axis=1)
    w_attn = lax.all_gather(attn_pack, "dp", axis=0, tiled=True)
    w_attn, mlp_pack = lax.optimization_barrier((w_attn, mlp_pack))
    w_mlp = lax.all_gather(mlp_pack, "dp", axis=0, tiled=True)
    w_qkv = w_attn[:, :qkv_cols]
    wo_t = w_attn[:, qkv_cols:]
    w_gu = w_mlp[:, : 2 * units]
    wd_t = w_mlp[:, 2 * units :]

    both = jnp.concatenate([layer_in, out_grad], axis=1)
    both = jnp.concatenate([both, swap(both)], axis=0)
    width = layer_in.shape[1]
    residual = both[:, :width].astype(f32)
    dy_full = both[:, width:]
    me = lax.axis_index("tensor")
    steps = jnp.arange(own, dtype=jnp.int32)
    slots = jnp.concatenate([me * own + steps, (1 - me) * own + steps])
    seg, pos = layout(seq_lengths[0], slots)
    inv = ROPE_BASE ** (-2.0 * jnp.arange(HEAD_SIZE // 2, dtype=f32) / HEAD_SIZE)
    angle = pos.astype(f32)[:, None] * inv[None, :]
    cosine = jnp.cos(angle)
    sine = jnp.sin(angle)
    allowed = (seg[:, None] == seg[None, :]) & (slots[None, :] <= slots[:, None])

    r_in = lax.rsqrt(jnp.mean(residual * residual, -1, keepdims=True) + EPS)
    a1_full = (residual * r_in * attn_gain).astype(bf)
    qkv = matrix_product(a1_full, w_qkv)
    q_raw = qkv[:, :q_cols]
    key_unrotated = qkv[:, q_cols : q_cols + k_cols]
    q_bf = (
        head_prep(q_raw, query_gain, cosine, sine, q_heads)
        .astype(bf)
        .reshape(count, kv_heads, group, HEAD_SIZE)
    )
    k_bf = head_prep(key_unrotated, key_gain, cosine, sine, kv_heads).astype(bf)
    v_bf = qkv[:, q_cols + k_cols :].astype(bf).reshape(count, kv_heads, HEAD_SIZE)

    raw = jnp.einsum("qhgd,khd->hgqk", q_bf, k_bf, preferred_element_type=f32) * scale
    masked = jnp.where(allowed, raw, NEG)
    top = jnp.max(masked, -1, keepdims=True)
    log_total = top + jnp.log(jnp.sum(jnp.exp(masked - top), -1, keepdims=True))
    probs = jnp.exp(masked - log_total)
    probs_bf = probs.astype(bf)
    attended = jnp.einsum("hgqk,khd->qhgd", probs_bf, v_bf, preferred_element_type=f32)
    attended_bf = attended.reshape(count, q_heads * HEAD_SIZE).astype(bf)
    attn_part = by_cols(attended_bf, wo_t).astype(bf)
    middle = residual + pair_sum(attn_part)

    r_mid = lax.rsqrt(jnp.mean(middle * middle, -1, keepdims=True) + EPS)
    a2_full = (middle * r_mid * mlp_gain).astype(bf)
    gate_up = matrix_product(a2_full, w_gu)
    gate = gate_up[:, :units]
    upward = gate_up[:, units:]
    sigma = jax.nn.sigmoid(gate)
    act = (gate * sigma * upward).astype(bf)
    d_act = matrix_product(dy_full, wd_t)
    d_gate = (d_act * upward * sigma * (1.0 + gate * (1.0 - sigma))).astype(bf)
    d_up = (d_act * gate * sigma).astype(bf)
    d_gate_up = jnp.concatenate([d_gate, d_up], axis=1)
    d_a2_part = by_cols(d_gate_up, w_gu).astype(bf)
    d_a2 = pair_sum(d_a2_part)
    mlp_grads = jnp.concatenate(
        [by_rows(a2_full, d_gate_up).astype(bf), by_rows(dy_full, act).astype(bf)], axis=1
    )
    mlp_grads = lax.psum_scatter(mlp_grads, "dp", scatter_dimension=0, tiled=True)

    mlp_part = by_cols(act, wd_t)
    mlp_sum = mlp_part[:own] + swap(mlp_part[own:].astype(bf)).astype(f32)
    layer_out = (middle[:own] + mlp_sum).astype(bf)

    scaled = d_a2 * mlp_gain
    d_middle = (
        dy_full.astype(f32)
        + r_mid * scaled
        - middle * (r_mid * r_mid * r_mid) * jnp.mean(scaled * middle, -1, keepdims=True)
    )
    mlp_gain_part = jnp.sum(d_a2[:own] * middle[:own] * r_mid[:own], 0)
    dh_full = d_middle.astype(bf)
    d_att = matrix_product(dh_full, wo_t).astype(bf).reshape(count, kv_heads, group, HEAD_SIZE)
    d_probs = jnp.einsum("qhgd,khd->hgqk", d_att, v_bf, preferred_element_type=f32)
    delta = jnp.sum(d_probs * probs, -1, keepdims=True)
    d_scores = (probs * (d_probs - delta)).astype(bf)
    d_q_rot = (
        jnp.einsum("hgqk,khd->qhgd", d_scores, k_bf, preferred_element_type=f32) * scale
    ).reshape(count, q_heads, HEAD_SIZE)
    d_k_rot = jnp.einsum("hgqk,qhgd->khd", d_scores, q_bf, preferred_element_type=f32) * scale
    d_v_raw = (
        jnp.einsum("hgqk,qhgd->khd", probs_bf, d_att, preferred_element_type=f32)
        .reshape(count, kv_heads * HEAD_SIZE)
        .astype(bf)
    )
    _, pull_query = jax.vjp(
        lambda raw, gain: head_prep(raw, gain, cosine, sine, q_heads), q_raw, query_gain
    )
    d_q_raw, query_gain_part = pull_query(d_q_rot)
    _, pull_key = jax.vjp(
        lambda raw, gain: head_prep(raw, gain, cosine, sine, kv_heads), key_unrotated, key_gain
    )
    d_k_raw, key_gain_part = pull_key(d_k_rot)
    d_qkv = jnp.concatenate([d_q_raw.astype(bf), d_k_raw.astype(bf), d_v_raw], axis=1)
    attn_grads = jnp.concatenate(
        [by_rows(a1_full, d_qkv).astype(bf), by_rows(dh_full, attended_bf).astype(bf)], axis=1
    )
    attn_grads = lax.psum_scatter(attn_grads, "dp", scatter_dimension=0, tiled=True)

    d_a1_part = by_cols(d_qkv, w_qkv)
    d_a1 = d_a1_part[:own] + swap(d_a1_part[own:].astype(bf)).astype(f32)
    x_own, r_own = residual[:own], r_in[:own]
    scaled = d_a1 * attn_gain
    input_grad = (
        d_middle[:own]
        + r_own * scaled
        - x_own * (r_own * r_own * r_own) * jnp.mean(scaled * x_own, -1, keepdims=True)
    ).astype(bf)
    attn_gain_part = jnp.sum(d_a1 * x_own * r_own, 0)
    gains = lax.psum(
        (attn_gain_part, query_gain_part, key_gain_part, mlp_gain_part), ("dp", "tensor")
    )
    attn_grads = attn_grads.astype(f32)
    mlp_grads = mlp_grads.astype(f32)
    return (
        layer_out,
        input_grad,
        gains[0],
        gains[1],
        gains[2],
        attn_grads[:, :q_cols],
        attn_grads[:, q_cols : q_cols + k_cols],
        attn_grads[:, q_cols + k_cols : qkv_cols],
        attn_grads[:, qkv_cols:].T,
        gains[3],
        mlp_grads[:, :units],
        mlp_grads[:, units : 2 * units],
        mlp_grads[:, 2 * units :].T,
    )


def solution(mesh):
    placed = (
        P(("dp", "tensor"), None),
        P("dp", None),
        P(),
        P(),
        P(),
        P("dp", "tensor"),
        P("dp", "tensor"),
        P("dp", "tensor"),
        P("tensor", "dp"),
        P(),
        P("dp", "tensor"),
        P("dp", "tensor"),
        P("tensor", "dp"),
        P(("dp", "tensor"), None),
    )
    return jax.shard_map(
        shards,
        mesh=mesh,
        in_specs=placed,
        out_specs=(
            P(("dp", "tensor"), None),
            P(("dp", "tensor"), None),
            P(),
            P(),
            P(),
            P("dp", "tensor"),
            P("dp", "tensor"),
            P("dp", "tensor"),
            P("tensor", "dp"),
            P(),
            P("dp", "tensor"),
            P("dp", "tensor"),
            P("tensor", "dp"),
        ),
        check_vma=False,
    )
```

time: 992 us -> 425 us (0.43)
  waiting for transfers between devices: 785 us -> 265 us
  blocking collectives: 82.9 us -> 40.7 us
  matrix products: 59.5 us -> 38.1 us
    reduce_scatter x11 -> x2, waiting for transfers between devices: 524 us -> 125 us  [the longest x1 110 us: shards(): lax.psum_scatter(mlp_grads, 'dp', scatter_dimension=0, tiled=True)]
    all_gather x7 -> x2, waiting for transfers between devices: 256 us -> 98 us  [the longest x1 64.3 us: shards(): w_attn = lax.all_gather(attn_pack, 'dp', axis=0, tiled=True)]
    all_gather x4 -> x0, blocking collectives: 43.3 us -> none  [the longest x1 16.1 us: shards(): dy_full = lax.all_gather(out_grad, 'tensor', axis=0, tiled=True)]
    ppermute x0 -> x5, waiting for transfers between devices: none -> 41.9 us  [swap(): return lax.ppermute(v, 'tensor', [(0, 1), (1, 0)])]
    dot_general x7 -> x4, matrix products: 20.3 us -> 6.38 us  [by_rows(): lax.dot_general(a, b, (((0,), (0,)), ((), ())), preferred_element_type=jn...]
    concatenate x0 -> x5, other arithmetic: none -> 11.6 us  [the longest x1 4.54 us: shards(): jnp.concatenate([by_rows(a2_full, d_gate_up).astype(bf), by_rows(dy_full,...]
    dot_general x7 -> x4, matrix products: 21.1 us -> 14.1 us  [matrix_product(): return jnp.dot(a, b, preferred_element_type=jnp.float32)]
  transfers between devices with their start and end apart: 18 -> 9, of which waited for: 16 -> 9; matrix products, arithmetic and copies ran while one was open for 6% -> 11% of each run, Pallas kernels for 0% -> 0%
where the time goes in v1:
time: 425 us; the launch traced here: 424 us
  waiting for transfers between devices  265 us (62%)
  blocking collectives  40.7 us (10%)
  matrix products  38.1 us (9%)
  other arithmetic  31.2 us (7%)
  local copies, waits for them, and re-layouts  27 us (6%)
  between operations  14.7 us (3%)
  starting transfers between devices  7.16 us (2%)
    reduce_scatter x1, waiting for transfers between devices, shards(): lax.psum_scatter(mlp_grads, 'dp', scatter_dimension=0, tiled=True)  110 us
    all_gather x1, waiting for transfers between devices, shards(): w_attn = lax.all_gather(attn_pack, 'dp', axis=0, tiled=True)  64.3 us
    ppermute x5, waiting for transfers between devices, swap(): return lax.ppermute(v, 'tensor', [(0, 1), (1, 0)])  41.9 us
    psum x1, blocking collectives, shards(): lax.psum((attn_gain_part, query_gain_part, key_gain_part, mlp_gain_part),...  40.7 us
    all_gather x1, waiting for transfers between devices, shards(): w_mlp = lax.all_gather(mlp_pack, 'dp', axis=0, tiled=True)  33.7 us
    reduce_scatter x1, waiting for transfers between devices, shards(): lax.psum_scatter(attn_grads, 'dp', scatter_dimension=0, tiled=True)  14.8 us
    dot_general x4, matrix products, matrix_product(): return jnp.dot(a, b, preferred_element_type=jnp.float32)  14.1 us
    dot_general x4, matrix products, by_cols(): lax.dot_general(a, b, (((1,), (1,)), ((), ())), preferred_element_type=jn...  11.3 us
  transfers between devices with their start and end apart: 9, of which 9 were waited for; matrix products, arithmetic and copies ran while one was open for 11% of the time, Pallas kernels for 0%

profile of v1, /device:TPU:0, one launch (start us, length us, event | category | flops | bytes accessed | tf_op | source)
XLA Modules:
  0.0 423.8 jit_solution(14591877865611106278)
XLA Ops:
  9.2 2.0 pad_maximum_fusion.6
  11.2 64.3 %all-gather.3.cloned.1.call-done = bf16[1024,3072]{1,0:T(8,128)(2,1)} async-done(((bf16[64,3072]{1,0:T(8,128)(2,1)}), bf16[1024,3072]{1,0:T(8,128)(2,1)}) %all-gather.3.cloned.1.call-update) | async-done | bytes 6291472 | tf_op jit(solution)/shard_map/all_gather | solution.py:94
  79.0 10.8 %collective-permute-done = bf16[128,2048]{1,0:T(8,128)(2,1)S(1)} collective-permute-done((bf16[128,2048]{1,0:T(8,128)(2,1)S(1)}, bf16[128,2048]{1,0:T(8,128)(2,1)S(1)}, u32[]{:S(2)}, u32[]{:S(2)}) %collective-permute-start) | collective-permute-done | bytes 524320 | tf_op jit(solution)/shard_map/ppermute | solution.py:28
  91.2 3.5 fusion.6
  103.3 2.0 fusion.70
  106.1 2.5 fusion.23
  110.3 11.9 %collective-permute-done.1 = bf16[256,1024]{1,0:T(8,128)(2,1)S(1)} collective-permute-done((bf16[256,1024]{1,0:T(8,128)(2,1)S(1)}, bf16[256,1024]{1,0:T(8,128)(2,1)S(1)}, u32[]{:S(2)}, u32[]{:S(2)}) %collective-permute-start.1) | collective-permute-done | bytes 524320 | tf_op jit(solution)/shard_map/ppermute | solution.py:28
  124.1 33.7 %all-gather.5.cloned.1.call-done = bf16[1024,4608]{1,0:T(8,128)(2,1)} async-done(((bf16[64,4608]{1,0:T(8,128)(2,1)}), bf16[1024,4608]{1,0:T(8,128)(2,1)}) %all-gather.5.cloned.1.call-update) | async-done | bytes 9437200 | tf_op jit(solution)/shard_map/all_gather | solution.py:96
  157.8 5.1 %fusion.2 = f32[256,3072]{1,0:T(8,128)S(1)} fusion(bf16[1024,4608]{1,0:T(8,128)(2,1)} %all-gather.5.cloned.1.call-done, f32[256,1024]{1,0:T(8,128)} %get-tuple-element.32, f32[1024]{0:T(1024)S(1)} %copy-done.46, f32[256]{0:T(256)} %get-tuple-element.61), kind=kOutput, calls=%fused_computation.5 | convolution fusion | flops 1611399168 | bytes 10490880 | tf_op jit(solution)/shard_map/dot_general | solution.py:52
  164.0 2.3 multiply_convert_fusion.1
  169.7 12.6 %collective-permute-done.3 = bf16[256,1024]{1,0:T(8,128)(2,1)S(1)} collective-permute-done((bf16[256,1024]{1,0:T(8,128)(2,1)S(1)}, bf16[256,1024]{1,0:T(8,128)(2,1)S(1)}, u32[]{:S(2)}, u32[]{:S(2)}) %collective-permute-start.3) | collective-permute-done | bytes 524320 | tf_op jit(solution)/shard_map/ppermute | solution.py:28
  184.9 3.1 fusion.26
  188.0 2.0 copy.218
  190.1 2.3 fusion.31
  195.7 2.1 convolution_convert_fusion.3
  211.3 3.2 pad_maximum_fusion.1
  219.6 4.5 %pad_maximum_fusion = bf16[1024,4608]{1,0:T(8,128)(2,1)} fusion(bf16[1024,1536]{1,0:T(8,128)(2,1)S(1)} %convolution_convert_fusion.1, bf16[1024,3072]{1,0:T(8,128)(2,1)S(1)} %convolution_convert_fusion), kind=kLoop, calls=%fused_computation | loop fusion | flops 18874368 | bytes 18874368 | tf_op jit(solution)/shard_map/concatenate | solution.py:154
  224.9 3.2 fusion.10
  229.7 3.8 fusion.4
  234.1 2.1 collective-permute-done.2
  237.1 4.4 %collective-permute-done.4 = bf16[128,1024]{1,0:T(8,128)(2,1)S(1)} collective-permute-done((bf16[128,1024]{1,0:T(8,128)(2,1)S(1)}, bf16[128,1024]{1,0:T(8,128)(2,1)S(1)}, u32[]{:S(2)}, u32[]{:S(2)}) %collective-permute-start.4) | collective-permute-done | bytes 262176 | tf_op jit(solution)/shard_map/ppermute | solution.py:28
  241.7 40.7 %all-reduce.4 = (f32[1024]{0:T(1024)}, f32[128]{0:T(128)}, f32[128]{0:T(128)}, f32[1024]{0:T(1024)}) all-reduce(f32[1024]{0:T(1024)S(1)} %get-tuple-element.17, f32[128]{0:T(128)S(1)} %copy-done.62, f32[128]{0:T(128)S(1)} %copy-done.61, f32[1024]{0:T(1024)S(1)} %get-tuple-element.42), channel_id=1, replica_groups=mesh['dp'=16,'tensor'=2] {'dp','tensor'}, use_global_device_ids=true, to_apply=%region_15.16 | all-reduce | flops 2304 | bytes 18432 | tf_op jit(solution)/shard_map/psum | solution.py:208
  284.3 14.8 %reduce-scatter.3.cloned.1.call-done = bf16[64,3072]{1,0:T(8,128)(2,1)} async-done(((bf16[1024,3072]{1,0:T(8,128)(2,1)}), bf16[64,3072]{1,0:T(8,128)(2,1)}) %reduce-scatter.3.cloned.1.call-update) | async-done | bytes 393232 | tf_op jit(solution)/shard_map/reduce_scatter | solution.py:196
  304.1 110.2 %reduce-scatter.5.cloned.1.call-done = bf16[64,4608]{1,0:T(8,128)(2,1)} async-done(((bf16[1024,4608]{1,0:T(8,128)(2,1)}), bf16[64,4608]{1,0:T(8,128)(2,1)}) %reduce-scatter.5.cloned.1.call-update) | async-done | bytes 589840 | tf_op jit(solution)/shard_map/reduce_scatter | solution.py:157
  (235 shorter events, 61.7 us)
Async XLA Ops:
  7.2 68.4 %copy-start.40 = (bf16[128,1024]{1,0:T(8,128)(2,1)S(1)}, bf16[128,1024]{1,0:T(8,128)(2,1)}, u32[]{:S(2)}) copy-start(bf16[128,1024]{1,0:T(8,128)(2,1)} %param.14) | copy-start | bytes 786436
  7.2 68.4 %copy-start.41 = (bf16[128,1024]{1,0:T(8,128)(2,1)S(1)}, bf16[128,1024]{1,0:T(8,128)(2,1)}, u32[]{:S(2)}) copy-start(bf16[128,1024]{1,0:T(8,128)(2,1)} %param.27) | copy-start | bytes 786436
  7.2 70.0 %copy-start.67 = (s32[1,4]{1,0:T(1,128)S(1)}, s32[1,4]{1,0:T(1,128)}, u32[]{:S(2)}) copy-start(s32[1,4]{1,0:T(1,128)} %param.15) | copy-start | bytes 52
  7.2 68.3 %all-gather.3.cloned.1.call-start = ((), (), s32[]{:S(2)}) async-start(), calls=%async_computation.2 | async-start | bytes 6684672 | tf_op jit(solution)/shard_map/all_gather | solution.py:94
  9.1 148.7 %all-gather.5.cloned.1.call-start = ((), (), s32[]{:S(2)}) async-start(), calls=%async_computation.3 | async-start | bytes 10027008 | tf_op jit(solution)/shard_map/all_gather | solution.py:96
  75.5 223.6 %reduce-scatter.3.cloned.1.call-start = ((), (), s32[]{:S(2)}) async-start(), calls=%async_computation.4 | async-start | bytes 6684672 | tf_op jit(solution)/shard_map/reduce_scatter | solution.py:196
  75.6 15.6 %copy-start.51 = (f32[1024]{0:T(1024)S(1)}, f32[1024]{0:T(1024)}, u32[]{:S(2)}) copy-start(f32[1024]{0:T(1024)} %param.16) | copy-start | bytes 12292
  75.6 19.1 %copy-start.10 = (bf16[128,2048]{1,0:T(8,128)(2,1)}, bf16[128,2048]{1,0:T(8,128)(2,1)S(1)}, u32[]{:S(2)}) copy-start(bf16[128,2048]{1,0:T(8,128)(2,1)S(1)} %constant_dynamic-update-slice_fusion) | copy-start | bytes 1572868
  75.6 14.2 %collective-permute-start = (bf16[128,2048]{1,0:T(8,128)(2,1)S(1)}, bf16[128,2048]{1,0:T(8,128)(2,1)S(1)}, u32[]{:S(2)}, u32[]{:S(2)}) collective-permute-start(bf16[128,2048]{1,0:T(8,128)(2,1)S(1)} %constant_dynamic-update-slice_fusion), channel_id=1, source_target_pairs={{0,1},{1,0},{2,3},{3,2},{4,5},{5,4},{6,7},{7,6},{8,9},{9,8},{10,11... | collective-permute-start | bytes 1572872 | tf_op jit(solution)/shard_map/ppermute | solution.py:28
  108.7 13.6 %copy-start.19 = (bf16[256,1024]{1,0:T(8,128)(2,1)S(1)}, bf16[256,1024]{1,0:T(8,128)(2,1)}, u32[]{:S(2)}) copy-start(bf16[256,1024]{1,0:T(8,128)(2,1)} %copy-done.18) | copy-start | bytes 1572868
  108.7 13.5 %collective-permute-start.1 = (bf16[256,1024]{1,0:T(8,128)(2,1)S(1)}, bf16[256,1024]{1,0:T(8,128)(2,1)S(1)}, u32[]{:S(2)}, u32[]{:S(2)}) collective-permute-start(bf16[256,1024]{1,0:T(8,128)(2,1)S(1)} %fusion.23), channel_id=1, source_target_pairs={{0,1},{1,0},{2,3},{3,2},{4,5},{5,4},{6,7},{7,6},{8,9},{9,8},{10,11... | collective-permute-start | bytes 1572872 | tf_op jit(solution)/shard_map/ppermute | solution.py:28
  122.3 35.5 %copy-start.46 = (f32[1024]{0:T(1024)S(1)}, f32[1024]{0:T(1024)}, u32[]{:S(2)}) copy-start(f32[1024]{0:T(1024)} %param.23) | copy-start | bytes 12292
  157.8 6.1 %copy-start.66 = (bf16[1024,4608]{1,0:T(8,128)(2,1)S(1)}, bf16[1024,4608]{1,0:T(8,128)(2,1)}, u32[]{:S(2)}) copy-start(bf16[1024,4608]{1,0:T(8,128)(2,1)} %all-gather.5.cloned.1.call-done) | copy-start | bytes 28311556
  168.1 14.3 %copy-start = (f32[256,1024]{1,0:T(8,128)S(1)}, f32[256,1024]{1,0:T(8,128)}, u32[]{:S(2)}) copy-start(f32[256,1024]{1,0:T(8,128)} %get-tuple-element.32) | copy-start | bytes 3145732
  168.1 14.2 %collective-permute-start.3 = (bf16[256,1024]{1,0:T(8,128)(2,1)S(1)}, bf16[256,1024]{1,0:T(8,128)(2,1)S(1)}, u32[]{:S(2)}, u32[]{:S(2)}) collective-permute-start(bf16[256,1024]{1,0:T(8,128)(2,1)S(1)} %fusion.20), channel_id=1, source_target_pairs={{0,1},{1,0},{2,3},{3,2},{4,5},{5,4},{6,7},{7,6},{8,9},{9,8},{10,11... | collective-permute-start | bytes 1572872 | tf_op jit(solution)/shard_map/ppermute | solution.py:28
  214.6 199.7 %reduce-scatter.5.cloned.1.call-start = ((), (), s32[]{:S(2)}) async-start(), calls=%async_computation.5 | async-start | bytes 10027008 | tf_op jit(solution)/shard_map/reduce_scatter | solution.py:157
  228.1 8.2 %copy-start.6 = (f32[256,1024]{1,0:T(8,128)S(1)}, f32[256,1024]{1,0:T(8,128)}, u32[]{:S(2)}) copy-start(f32[256,1024]{1,0:T(8,128)} %copy-done.5) | copy-start | bytes 3145732
  228.1 8.2 %collective-permute-start.2 = (bf16[128,1024]{1,0:T(8,128)(2,1)S(1)}, bf16[128,1024]{1,0:T(8,128)(2,1)S(1)}, u32[]{:S(2)}, u32[]{:S(2)}) collective-permute-start(bf16[128,1024]{1,0:T(8,128)(2,1)S(1)} %slice.262), channel_id=1, source_target_pairs={{0,1},{1,0},{2,3},{3,2},{4,5},{5,4},{6,7},{7,6},{8,9},{9,8},{10,11... | collective-permute-start | bytes 786440 | tf_op jit(solution)/shard_map/ppermute | solution.py:28
  233.5 8.0 %copy-start.32 = (f32[256,1024]{1,0:T(8,128)}, f32[256,1024]{1,0:T(8,128)S(1)}, u32[]{:S(2)}) copy-start(f32[256,1024]{1,0:T(8,128)S(1)} %fusion.4) | copy-start | bytes 3145732
  233.5 8.0 %copy-start.22 = (f32[256,1024]{1,0:T(8,128)S(1)}, f32[256,1024]{1,0:T(8,128)}, u32[]{:S(2)}) copy-start(f32[256,1024]{1,0:T(8,128)} %get-tuple-element.27) | copy-start | bytes 3145732
  233.5 8.2 %copy-start.61 = (f32[128]{0:T(128)S(1)}, f32[128]{0:T(128)}, u32[]{:S(2)}) copy-start(f32[128]{0:T(128)} %get-tuple-element.21) | copy-start | bytes 1540
  233.5 8.2 %copy-start.62 = (f32[128]{0:T(128)S(1)}, f32[128]{0:T(128)}, u32[]{:S(2)}) copy-start(f32[128]{0:T(128)} %get-tuple-element.19) | copy-start | bytes 1540
  233.5 48.9 %copy-start.9 = (f32[256,1024]{1,0:T(8,128)S(1)}, f32[256,1024]{1,0:T(8,128)}, u32[]{:S(2)}) copy-start(f32[256,1024]{1,0:T(8,128)} %copy-done.7) | copy-start | bytes 3145732
  233.5 7.9 %collective-permute-start.4 = (bf16[128,1024]{1,0:T(8,128)(2,1)S(1)}, bf16[128,1024]{1,0:T(8,128)(2,1)S(1)}, u32[]{:S(2)}, u32[]{:S(2)}) collective-permute-start(bf16[128,1024]{1,0:T(8,128)(2,1)S(1)} %slice.261), channel_id=1, source_target_pairs={{0,1},{1,0},{2,3},{3,2},{4,5},{5,4},{6,7},{7,6},{8,9},{9,8},{10,11... | collective-permute-start | bytes 786440 | tf_op jit(solution)/shard_map/ppermute | solution.py:28
  (53 other events, 103.9 us)
Sparse Core Ops, SparseCore 0:
  10.9 64.5 all-gather.2
  77.8 80.0 all-gather.4
  214.7 84.3 reduce-scatter.2
  303.6 110.6 reduce-scatter.4

commit v2 on v1

--- a/solution.py
+++ b/solution.py
@@ -92,15 +92,15 @@
     )
     mlp_pack = jnp.concatenate([gate_weight, up_weight, down_weight.T], axis=1)
     w_attn = lax.all_gather(attn_pack, "dp", axis=0, tiled=True)
-    w_attn, mlp_pack = lax.optimization_barrier((w_attn, mlp_pack))
+
+    both = jnp.concatenate([layer_in, out_grad], axis=1)
+    both = jnp.concatenate([both, swap(both)], axis=0)
+    w_attn, mlp_pack, both = lax.optimization_barrier((w_attn, mlp_pack, both))
     w_mlp = lax.all_gather(mlp_pack, "dp", axis=0, tiled=True)
     w_qkv = w_attn[:, :qkv_cols]
     wo_t = w_attn[:, qkv_cols:]
     w_gu = w_mlp[:, : 2 * units]
     wd_t = w_mlp[:, 2 * units :]
-
-    both = jnp.concatenate([layer_in, out_grad], axis=1)
-    both = jnp.concatenate([both, swap(both)], axis=0)
     width = layer_in.shape[1]
     residual = both[:, :width].astype(f32)
     dy_full = both[:, width:]
@@ -154,6 +154,7 @@
     mlp_grads = jnp.concatenate(
         [by_rows(a2_full, d_gate_up).astype(bf), by_rows(dy_full, act).astype(bf)], axis=1
     )
+    d_a2, mlp_grads = lax.optimization_barrier((d_a2, mlp_grads))
     mlp_grads = lax.psum_scatter(mlp_grads, "dp", scatter_dimension=0, tiled=True)
 
     mlp_part = by_cols(act, wd_t)

time: 425 us -> 430 us (1.012)
  waiting for transfers between devices: 265 us -> 271 us
    all_gather x1, waiting for transfers between devices: 33.7 us -> 49.2 us  [shards(): w_mlp = lax.all_gather(mlp_pack, 'dp', axis=0, tiled=True)]
    all_gather x1, waiting for transfers between devices: 64.3 us -> 49.2 us  [shards(): w_attn = lax.all_gather(attn_pack, 'dp', axis=0, tiled=True)]
    reduce_scatter x1, waiting for transfers between devices: 14.8 us -> 24.5 us  [shards(): lax.psum_scatter(attn_grads, 'dp', scatter_dimension=0, tiled=True)]
    ppermute x5, waiting for transfers between devices: 41.9 us -> 37.4 us  [swap(): return lax.ppermute(v, 'tensor', [(0, 1), (1, 0)])]
    unnamed x142 -> x138, local copies, waits for them, and re-layouts: 10.9 us -> 10.2 us
  transfers between devices with their start and end apart: 9 -> 9, of which waited for: 9 -> 9; matrix products, arithmetic and copies ran while one was open for 11% -> 9% of each run, Pallas kernels for 0% -> 0%
where the time goes in v2:
time: 430 us; the launch traced here: 429 us
  waiting for transfers between devices  271 us (63%)
  blocking collectives  40.6 us (9%)
  matrix products  36.9 us (9%)
  other arithmetic  29.4 us (7%)
  local copies, waits for them, and re-layouts  27.5 us (6%)
  between operations  15 us (3%)
  starting transfers between devices  8.68 us (2%)
    reduce_scatter x1, waiting for transfers between devices, shards(): lax.psum_scatter(mlp_grads, 'dp', scatter_dimension=0, tiled=True)  110 us
    all_gather x1, waiting for transfers between devices, shards(): w_attn = lax.all_gather(attn_pack, 'dp', axis=0, tiled=True)  49.2 us
    all_gather x1, waiting for transfers between devices, shards(): w_mlp = lax.all_gather(mlp_pack, 'dp', axis=0, tiled=True)  49.2 us
    psum x1, blocking collectives, shards(): lax.psum((attn_gain_part, query_gain_part, key_gain_part, mlp_gain_part),...  40.6 us
    ppermute x5, waiting for transfers between devices, swap(): return lax.ppermute(v, 'tensor', [(0, 1), (1, 0)])  37.4 us
    reduce_scatter x1, waiting for transfers between devices, shards(): lax.psum_scatter(attn_grads, 'dp', scatter_dimension=0, tiled=True)  24.5 us
    dot_general x4, matrix products, matrix_product(): return jnp.dot(a, b, preferred_element_type=jnp.float32)  13.4 us
    dot_general x4, matrix products, by_cols(): lax.dot_general(a, b, (((1,), (1,)), ((), ())), preferred_element_type=jn...  12 us
  transfers between devices with their start and end apart: 9, of which 9 were waited for; matrix products, arithmetic and copies ran while one was open for 9% of the time, Pallas kernels for 0%

profile of v2, /device:TPU:0, one launch (start us, length us, event | category | flops | bytes accessed | tf_op | source)
XLA Modules:
  0.0 428.7 jit_solution(6239537780341975282)
XLA Ops:
  11.2 3.0 collective-permute-start
  15.2 11.0 %collective-permute-done = bf16[128,2048]{1,0:T(8,128)(2,1)S(1)} collective-permute-done((bf16[128,2048]{1,0:T(8,128)(2,1)S(1)}, bf16[128,2048]{1,0:T(8,128)(2,1)S(1)}, u32[]{:S(2)}, u32[]{:S(2)}) %collective-permute-start) | collective-permute-done | bytes 524320 | tf_op jit(solution)/shard_map/ppermute | solution.py:28
  26.2 49.2 %all-gather.3.cloned.1.call-done = bf16[1024,3072]{1,0:T(8,128)(2,1)} async-done(((bf16[64,3072]{1,0:T(8,128)(2,1)}), bf16[1024,3072]{1,0:T(8,128)(2,1)}) %all-gather.3.cloned.1.call-update) | async-done | bytes 6291472 | tf_op jit(solution)/shard_map/all_gather | solution.py:94
  77.6 3.5 fusion.6
  90.0 2.5 fusion.23
  94.1 12.6 %collective-permute-done.1 = bf16[256,1024]{1,0:T(8,128)(2,1)S(1)} collective-permute-done((bf16[256,1024]{1,0:T(8,128)(2,1)S(1)}, bf16[256,1024]{1,0:T(8,128)(2,1)S(1)}, u32[]{:S(2)}, u32[]{:S(2)}) %collective-permute-start.1) | collective-permute-done | bytes 524320 | tf_op jit(solution)/shard_map/ppermute | solution.py:28
  108.6 49.2 %all-gather.5.cloned.1.call-done = bf16[1024,4608]{1,0:T(8,128)(2,1)} async-done(((bf16[64,4608]{1,0:T(8,128)(2,1)}), bf16[1024,4608]{1,0:T(8,128)(2,1)}) %all-gather.5.cloned.1.call-update) | async-done | bytes 9437200 | tf_op jit(solution)/shard_map/all_gather | solution.py:99
  157.8 5.1 %fusion.2 = f32[256,3072]{1,0:T(8,128)S(1)} fusion(bf16[1024,4608]{1,0:T(8,128)(2,1)} %all-gather.5.cloned.1.call-done, f32[256,1024]{1,0:T(8,128)} %get-tuple-element.34, f32[1024]{0:T(1024)S(1)} %copy-done.46, f32[256]{0:T(256)} %get-tuple-element.63), kind=kOutput, calls=%fused_computation.5 | convolution fusion | flops 1611399168 | bytes 10490880 | tf_op jit(solution)/shard_map/dot_general | solution.py:52
  167.7 2.7 fusion.20
  172.9 4.6 %pad_maximum_fusion = bf16[1024,4608]{1,0:T(8,128)(2,1)} fusion(bf16[1024,1536]{1,0:T(8,128)(2,1)S(1)} %convolution_convert_fusion.1, bf16[1024,3072]{1,0:T(8,128)(2,1)S(1)} %convolution_convert_fusion), kind=kLoop, calls=%fused_computation | loop fusion | flops 18874368 | bytes 18874368 | tf_op jit(solution)/shard_map/concatenate | solution.py:154
  177.4 7.3 %collective-permute-done.3 = bf16[256,1024]{1,0:T(8,128)(2,1)} collective-permute-done((bf16[256,1024]{1,0:T(8,128)(2,1)}, bf16[256,1024]{1,0:T(8,128)(2,1)}, u32[]{:S(2)}, u32[]{:S(2)}) %collective-permute-start.3) | collective-permute-done | bytes 524320 | tf_op jit(solution)/shard_map/ppermute | solution.py:28
  189.2 3.2 fusion.26
  192.4 2.0 copy.218
  194.5 2.3 fusion.31
  200.1 2.1 convolution_convert_fusion.3
  203.9 2.5 copy.216
  213.1 2.2 fusion.32
  217.2 3.3 pad_maximum_fusion.1
  221.7 3.0 fusion.10
  226.3 3.8 fusion.4
  233.6 4.4 %collective-permute-done.4 = bf16[128,1024]{1,0:T(8,128)(2,1)S(1)} collective-permute-done((bf16[128,1024]{1,0:T(8,128)(2,1)S(1)}, bf16[128,1024]{1,0:T(8,128)(2,1)S(1)}, u32[]{:S(2)}, u32[]{:S(2)}) %collective-permute-start.4) | collective-permute-done | bytes 262176 | tf_op jit(solution)/shard_map/ppermute | solution.py:28
  238.2 40.6 %all-reduce.4 = (f32[1024]{0:T(1024)}, f32[128]{0:T(128)}, f32[128]{0:T(128)}, f32[1024]{0:T(1024)}) all-reduce(f32[1024]{0:T(1024)S(1)} %get-tuple-element.23, f32[128]{0:T(128)S(1)} %get-tuple-element.25, f32[128]{0:T(128)S(1)} %copy-done.61, f32[1024]{0:T(1024)S(1)} %get-tuple-element.44), channel_id=1, replica_groups=mesh['dp'=16,'tensor'=2] {'dp','tensor'}, use_global_device_ids=true, to_apply=%region_15.16 | all-reduce | flops 2304 | bytes 18432 | tf_op jit(solution)/shard_map/psum | solution.py:209
  279.7 24.5 %reduce-scatter.3.cloned.1.call-done = bf16[64,3072]{1,0:T(8,128)(2,1)} async-done(((bf16[1024,3072]{1,0:T(8,128)(2,1)}), bf16[64,3072]{1,0:T(8,128)(2,1)}) %reduce-scatter.3.cloned.1.call-update) | async-done | bytes 393232 | tf_op jit(solution)/shard_map/reduce_scatter | solution.py:197
  309.2 110.1 %reduce-scatter.5.cloned.1.call-done = bf16[64,4608]{1,0:T(8,128)(2,1)} async-done(((bf16[1024,4608]{1,0:T(8,128)(2,1)}), bf16[64,4608]{1,0:T(8,128)(2,1)}) %reduce-scatter.5.cloned.1.call-update) | async-done | bytes 589840 | tf_op jit(solution)/shard_map/reduce_scatter | solution.py:158
  (233 shorter events, 59.0 us)
Async XLA Ops:
  7.2 7.1 %copy-start.43 = (bf16[1536,64]{0,1:T(8,128)(2,1)S(1)}, bf16[1536,64]{0,1:T(8,128)(2,1)}, u32[]{:S(2)}) copy-start(bf16[1536,64]{0,1:T(8,128)(2,1)} %param.26) | copy-start | bytes 589828
  7.2 7.1 %copy-start.44 = (bf16[64,1536]{1,0:T(8,128)(2,1)S(1)}, bf16[64,1536]{1,0:T(8,128)(2,1)}, u32[]{:S(2)}) copy-start(bf16[64,1536]{1,0:T(8,128)(2,1)} %param.25) | copy-start | bytes 589828
  7.2 7.0 %copy-start.45 = (bf16[64,1536]{1,0:T(8,128)(2,1)S(1)}, bf16[64,1536]{1,0:T(8,128)(2,1)}, u32[]{:S(2)}) copy-start(bf16[64,1536]{1,0:T(8,128)(2,1)} %param.24) | copy-start | bytes 589828
  7.2 68.3 %all-gather.3.cloned.1.call-start = ((), (), s32[]{:S(2)}) async-start(), calls=%async_computation.2 | async-start | bytes 6684672 | tf_op jit(solution)/shard_map/all_gather | solution.py:94
  9.2 148.6 %all-gather.5.cloned.1.call-start = ((), (), s32[]{:S(2)}) async-start(), calls=%async_computation.3 | async-start | bytes 10027008 | tf_op jit(solution)/shard_map/all_gather | solution.py:99
  10.2 65.3 %copy-start.65 = (s32[1,4]{1,0:T(1,128)S(1)}, s32[1,4]{1,0:T(1,128)}, u32[]{:S(2)}) copy-start(s32[1,4]{1,0:T(1,128)} %param.15) | copy-start | bytes 52
  11.2 15.0 %collective-permute-start = (bf16[128,2048]{1,0:T(8,128)(2,1)S(1)}, bf16[128,2048]{1,0:T(8,128)(2,1)S(1)}, u32[]{:S(2)}, u32[]{:S(2)}) collective-permute-start(bf16[128,2048]{1,0:T(8,128)(2,1)S(1)} %constant_dynamic-update-slice_fusion), channel_id=1, source_target_pairs={{0,1},{1,0},{2,3},{3,2},{4,5},{5,4},{6,7},{7,6},{8,9},{9,8},{10,11... | collective-permute-start | bytes 1572872 | tf_op jit(solution)/shard_map/ppermute | solution.py:28
  14.2 63.3 %copy-start.51 = (f32[1024]{0:T(1024)S(1)}, f32[1024]{0:T(1024)}, u32[]{:S(2)}) copy-start(f32[1024]{0:T(1024)} %param.16) | copy-start | bytes 12292
  26.2 54.8 %copy-start.3 = (bf16[256,2048]{1,0:T(8,128)(2,1)}, bf16[256,2048]{1,0:T(8,128)(2,1)S(1)}, u32[]{:S(2)}) copy-start(bf16[256,2048]{1,0:T(8,128)(2,1)S(1)} %pad_maximum_fusion.3) | copy-start | bytes 3145732
  75.5 228.7 %reduce-scatter.3.cloned.1.call-start = ((), (), s32[]{:S(2)}) async-start(), calls=%async_computation.4 | async-start | bytes 6684672 | tf_op jit(solution)/shard_map/reduce_scatter | solution.py:197
  92.5 14.3 %copy-start.4 = (bf16[256,2048]{1,0:T(8,128)(2,1)S(1)}, bf16[256,2048]{1,0:T(8,128)(2,1)}, u32[]{:S(2)}) copy-start(bf16[256,2048]{1,0:T(8,128)(2,1)} %copy-done.3) | copy-start | bytes 3145732
  92.5 14.2 %collective-permute-start.1 = (bf16[256,1024]{1,0:T(8,128)(2,1)S(1)}, bf16[256,1024]{1,0:T(8,128)(2,1)S(1)}, u32[]{:S(2)}, u32[]{:S(2)}) collective-permute-start(bf16[256,1024]{1,0:T(8,128)(2,1)S(1)} %fusion.23), channel_id=1, source_target_pairs={{0,1},{1,0},{2,3},{3,2},{4,5},{5,4},{6,7},{7,6},{8,9},{9,8},{10,11... | collective-permute-start | bytes 1572872 | tf_op jit(solution)/shard_map/ppermute | solution.py:28
  106.8 51.0 %copy-start.46 = (f32[1024]{0:T(1024)S(1)}, f32[1024]{0:T(1024)}, u32[]{:S(2)}) copy-start(f32[1024]{0:T(1024)} %param.23) | copy-start | bytes 12292
  157.8 6.1 %copy-start.64 = (bf16[1024,4608]{1,0:T(8,128)(2,1)S(1)}, bf16[1024,4608]{1,0:T(8,128)(2,1)}, u32[]{:S(2)}) copy-start(bf16[1024,4608]{1,0:T(8,128)(2,1)} %all-gather.5.cloned.1.call-done) | copy-start | bytes 28311556
  165.5 6.3 %copy-start.34 = (bf16[256,1536]{1,0:T(8,128)(2,1)}, bf16[256,1536]{1,0:T(8,128)(2,1)S(1)}, u32[]{:S(2)}) copy-start(bf16[256,1536]{1,0:T(8,128)(2,1)S(1)} %get-tuple-element.37) | copy-start | bytes 2359300
  170.4 14.4 %collective-permute-start.3 = (bf16[256,1024]{1,0:T(8,128)(2,1)}, bf16[256,1024]{1,0:T(8,128)(2,1)}, u32[]{:S(2)}, u32[]{:S(2)}) collective-permute-start(bf16[256,1024]{1,0:T(8,128)(2,1)} %fusion.20), channel_id=1, source_target_pairs={{0,1},{1,0},{2,3},{3,2},{4,5},{5,4},{6,7},{7,6},{8,9},{9,8},{10,11... | collective-permute-start | bytes 1572872 | tf_op jit(solution)/shard_map/ppermute | solution.py:28
  177.4 9.8 %copy-start.1 = (f32[256,1024]{1,0:T(8,128)S(1)}, f32[256,1024]{1,0:T(8,128)}, u32[]{:S(2)}) copy-start(f32[256,1024]{1,0:T(8,128)} %get-tuple-element.34) | copy-start | bytes 3145732
  220.5 198.7 %reduce-scatter.5.cloned.1.call-start = ((), (), s32[]{:S(2)}) async-start(), calls=%async_computation.5 | async-start | bytes 10027008 | tf_op jit(solution)/shard_map/reduce_scatter | solution.py:158
  224.7 8.1 %copy-start.2 = (f32[256,1024]{1,0:T(8,128)S(1)}, f32[256,1024]{1,0:T(8,128)}, u32[]{:S(2)}) copy-start(f32[256,1024]{1,0:T(8,128)} %get-tuple-element.34) | copy-start | bytes 3145732
  224.7 8.1 %copy-start.9 = (f32[256,1024]{1,0:T(8,128)S(1)}, f32[256,1024]{1,0:T(8,128)}, u32[]{:S(2)}) copy-start(f32[256,1024]{1,0:T(8,128)} %copy-done.8) | copy-start | bytes 3145732
  224.7 8.1 %collective-permute-start.2 = (bf16[128,1024]{1,0:T(8,128)(2,1)S(1)}, bf16[128,1024]{1,0:T(8,128)(2,1)S(1)}, u32[]{:S(2)}, u32[]{:S(2)}) collective-permute-start(bf16[128,1024]{1,0:T(8,128)(2,1)S(1)} %slice.260), channel_id=1, source_target_pairs={{0,1},{1,0},{2,3},{3,2},{4,5},{5,4},{6,7},{7,6},{8,9},{9,8},{10,11... | collective-permute-start | bytes 786440 | tf_op jit(solution)/shard_map/ppermute | solution.py:28
  230.0 8.2 %copy-start.61 = (f32[128]{0:T(128)S(1)}, f32[128]{0:T(128)}, u32[]{:S(2)}) copy-start(f32[128]{0:T(128)} %get-tuple-element.27) | copy-start | bytes 1540
  230.1 48.8 %copy-start.16 = (f32[256,1024]{1,0:T(8,128)S(1)}, f32[256,1024]{1,0:T(8,128)}, u32[]{:S(2)}) copy-start(f32[256,1024]{1,0:T(8,128)} %copy-done.14) | copy-start | bytes 3145732
  230.1 7.9 %collective-permute-start.4 = (bf16[128,1024]{1,0:T(8,128)(2,1)S(1)}, bf16[128,1024]{1,0:T(8,128)(2,1)S(1)}, u32[]{:S(2)}, u32[]{:S(2)}) collective-permute-start(bf16[128,1024]{1,0:T(8,128)(2,1)S(1)} %slice.259), channel_id=1, source_target_pairs={{0,1},{1,0},{2,3},{3,2},{4,5},{5,4},{6,7},{7,6},{8,9},{9,8},{10,11... | collective-permute-start | bytes 786440 | tf_op jit(solution)/shard_map/ppermute | solution.py:28
  (51 other events, 98.3 us)
Sparse Core Ops, SparseCore 0:
  10.9 64.5 all-gather.2
  77.8 80.0 all-gather.4
  220.6 83.5 reduce-scatter.2
  308.7 110.4 reduce-scatter.4
